TPU v7x, 768 devices: a whole 4x8x12 slice. The times are simulated.
768 devices in a mesh: store: 64 (over y, x, core), grp: 12 (over z).
Axes of the slice: x: 4, y: 8, z: 12, core: 2. Of those that a mesh axis runs over, the one named last changes fastest.
Arguments:
- layer_input: bfloat16 [12, 64, 128, 1024], P('grp', 'store'), may hold values from -6 to 6
- initial: bfloat16 [12, 64, 128, 1024], P('grp', 'store'), may hold values from -6 to 6
- history: bfloat16 [2, 12, 8192, 1024], P(None, 'grp', 'store'), may hold values from -6 to 6
- batch_ids: int32 [12, 64, 64, 2], P('grp', 'store'), may hold values from 0 to 127, as said below
- batch_count: int32 [12, 64, 64], P('grp', 'store'), may hold values from 1 to 2, as said below
- halo_ids: int32 [12, 64, 64, 2], P('grp', 'store'), may hold values from 0 to 127, as said below
- halo_count: int32 [12, 64, 64], P('grp', 'store'), may hold values from 1 to 2, as said below
- block_cols: int32 [12, 64, 2, 4], P('grp', 'store'), may hold values from 0 to 3, all different within a row
- block_vals: bfloat16 [12, 64, 2, 4, 64, 64], P('grp', 'store'), may hold values from -0.375 to 0.375
- weight_one: bfloat16 [1024, 1024], replicated, may hold values from -0.1875 to 0.1875
- weight_two: bfloat16 [1024, 1024], replicated, may hold values from -0.1875 to 0.1875
- cotangent: bfloat16 [12, 64, 128, 1024], P('grp', 'store'), may hold values from -6 to 6
Outputs:
- new_history: bfloat16 [2, 12, 8192, 1024], P(None, 'grp', 'store')
- grad_two: float32 [1024, 1024], P('store')
Inputs may be any that keep to these rules, and one draw needn't show every extreme that they name: `batch_ids`: within one group the batch slots of all devices name each owner's rows at most once. `batch_count`: in each group one owner has all 2 slots live from every device. `halo_ids`: the rows one device names of one owner are distinct. `halo_count`: in each group one owner has all 2 slots live from every device.
All inputs are finite; a program needn't handle non-finite values.
Results may differ from a plain program's by a relative error of at most 0.0054.
Values may be sent and summed in bfloat16 or wider, within the bound.
A program may use at most 64 MiB of HBM per device.

v0:
```python
import math

import jax
import jax.numpy as jnp
from jax import lax
from jax.sharding import PartitionSpec as P

ALPHA = 0.1
BETA_ONE = math.log(1.5)
BETA_TWO = math.log(1.25)


def slot_mask(counts, slots_per):
    slot_index = jnp.arange(slots_per, dtype=jnp.int32)[None, :]
    return (slot_index < counts[:, None]).reshape(-1)


def spread(col_blocks, block_values, fresh):
    blocks = fresh.reshape(-1, block_values.shape[2], fresh.shape[1])
    picked = blocks[col_blocks]
    aggregate = jnp.einsum(
        "rkij,rkjh->rih", block_values, picked, preferred_element_type=jnp.float32
    )
    return aggregate.reshape(-1, fresh.shape[1])


def gcn_layer(
    layer_rows, pulled, batch_live, halo_live, initial, col_blocks, block_values, weight, mixing
):
    fresh = jnp.concatenate(
        [
            jnp.where(batch_live[:, None], layer_rows, jnp.zeros_like(layer_rows)),
            jnp.where(halo_live[:, None], pulled, jnp.zeros_like(pulled)),
        ],
        axis=0,
    )
    aggregate = spread(col_blocks, block_values, fresh)
    support = ((1.0 - ALPHA) * aggregate + ALPHA * initial.astype(jnp.float32)).astype(jnp.bfloat16)
    preact = (1.0 - mixing) * support.astype(jnp.float32) + mixing * jnp.dot(
        support, weight, preferred_element_type=jnp.float32
    )
    return (support, preact)


def gelu_tanh(pre_act):
    return jax.nn.gelu(pre_act, approximate=True)


def per_device(
    layer_input,
    initial,
    history,
    batch_ids,
    batch_count,
    halo_ids,
    halo_count,
    block_cols,
    block_vals,
    weight_one,
    weight_two,
    cotangent,
):
    rows_in = layer_input[0, 0]
    first_rows = initial[0, 0]
    history_shard = history[:, 0]
    col_blocks = block_cols[0, 0]
    block_values = block_vals[0, 0]
    cotan_rows = cotangent[0, 0]
    halo_wanted = halo_ids[0, 0]
    store_count = lax.axis_size("store")
    batch_rows = rows_in.shape[0]
    features = rows_in.shape[1]
    per_owner = batch_rows // store_count
    halo_slots = halo_wanted.shape[1]
    batch_live = slot_mask(batch_count[0, 0], per_owner)
    halo_live = slot_mask(halo_count[0, 0], halo_slots)
    targets = jnp.where(batch_live.reshape(store_count, per_owner), batch_ids[0, 0], batch_rows)

    def fetch_layer(which_layer):
        found = jnp.take(
            history_shard[which_layer],
            lax.all_to_all(halo_wanted, "store", split_axis=0, concat_axis=0, tiled=True),
            axis=0,
        )
        received = lax.all_to_all(found, "store", split_axis=0, concat_axis=0, tiled=True)
        return received.reshape(-1, features)

    def place(layer_rows, arrived, target_rows):
        return layer_rows.at[target_rows].set(arrived, mode="drop")

    def push_layer(layer_rows, which_layer):
        arrived, target_rows = (
            lax.all_to_all(
                layer_rows.reshape(store_count, per_owner, features),
                "store",
                split_axis=0,
                concat_axis=0,
                tiled=True,
            ),
            lax.all_to_all(targets, "store", split_axis=0, concat_axis=0, tiled=True),
        )
        return place(
            history_shard[which_layer], arrived.reshape(-1, features), target_rows.reshape(-1)
        )

    pulled_one = fetch_layer(0)
    pulled_two = None
    history_zero = push_layer(rows_in, 0)
    support_one, preact_one = gcn_layer(
        rows_in,
        pulled_one,
        batch_live,
        halo_live,
        first_rows,
        col_blocks,
        block_values,
        weight_one,
        BETA_ONE,
    )
    fresh_one = gelu_tanh(preact_one).astype(jnp.bfloat16)
    history_one = push_layer(fresh_one, 1)
    pulled_two = fetch_layer(1)
    support_two, preact_two = gcn_layer(
        fresh_one,
        pulled_two,
        batch_live,
        halo_live,
        first_rows,
        col_blocks,
        block_values,
        weight_two,
        BETA_TWO,
    )
    unused, pull_back = jax.vjp(gelu_tanh, preact_two)
    grad_pre = jnp.where(
        batch_live[:, None], pull_back(cotan_rows.astype(jnp.float32))[0], 0.0
    ).astype(jnp.bfloat16)
    factor = BETA_TWO / math.sqrt(lax.axis_size("grp") * store_count * batch_rows)
    left_rows, right_rows = (support_two, grad_pre)
    partial_sum = lax.psum_scatter(
        factor
        * lax.dot_general(
            left_rows, right_rows, (((0,), (0,)), ((), ())), preferred_element_type=jnp.float32
        ),
        "store",
        scatter_dimension=0,
        tiled=True,
    )
    gradient = lax.psum(partial_sum, "grp")
    new_history = jnp.stack([history_zero, history_one])[:, None]
    return (new_history, gradient)


def solution(mesh):
    in_specs = (
        P("grp", "store", None, None),
        P("grp", "store", None, None),
        P(None, "grp", "store", None),
        P("grp", "store", None, None),
        P("grp", "store", None),
        P("grp", "store", None, None),
        P("grp", "store", None),
        P("grp", "store", None, None),
        P("grp", "store", None, None, None, None),
        P(),
        P(),
        P("grp", "store", None, None),
    )
    out_specs = (P(None, "grp", "store", None), P("store", None))
    return jax.shard_map(
        per_device, mesh=mesh, in_specs=in_specs, out_specs=out_specs, check_vma=False
    )
```

profile of v0, /device:TPU:6, one launch (start us, length us, event | category | flops | bytes accessed | tf_op | source)
XLA Modules:
  0.0 367.1 jit_solution(8590019993382530830)
XLA Ops:
  7.2 1.5 copy.27
  8.7 13.5 %all-to-all-start.2 = ((s32[64,1,2]{2,1,0:T(1,128)}), s32[64,1,2]{2,1,0:T(1,128)S(1)}, u32[]{:S(2)}, u32[]{:S(2)}) async-start(s32[64,1,2]{2,1,0:T(1,128)} %copy.27), calls=%async_computation.2 | async-start | bytes 65536 | tf_op jit(solution)/shard_map/all_to_all | solution.py:82
  23.3 6.8 %all-to-all-done.2 = s32[64,1,2]{2,1,0:T(1,128)S(1)} async-done(((s32[64,1,2]{2,1,0:T(1,128)}), s32[64,1,2]{2,1,0:T(1,128)S(1)}, u32[]{:S(2)}, u32[]{:S(2)}) %all-to-all-start.2) | async-done | bytes 544 | tf_op jit(solution)/shard_map/all_to_all | solution.py:82
  33.3 2.3 broadcast_select_fusion
  35.6 6.3 %all-to-all-start.5 = ((bf16[64,2,1024]{2,1,0:T(2,128)(2,1)}), bf16[64,2,1024]{2,1,0:T(2,128)(2,1)S(1)}, u32[]{:S(2)}, u32[]{:S(2)}) async-start(bf16[64,2,1024]{2,1,0:T(2,128)(2,1)} %get-tuple-element.11), calls=%async_computation.5 | async-start | bytes 524288 | tf_op jit(solution)/shard_map/all_to_all | solution.py:85
  42.2 11.7 %all-to-all-done.5 = bf16[64,2,1024]{2,1,0:T(2,128)(2,1)S(1)} async-done(((bf16[64,2,1024]{2,1,0:T(2,128)(2,1)}), bf16[64,2,1024]{2,1,0:T(2,128)(2,1)S(1)}, u32[]{:S(2)}, u32[]{:S(2)}) %all-to-all-start.5) | async-done | bytes 262176 | tf_op jit(solution)/shard_map/all_to_all | solution.py:85
  53.9 5.9 %all-to-all-start.3 = ((bf16[64,2,1024]{2,1,0:T(2,128)(2,1)}), bf16[64,2,1024]{2,1,0:T(2,128)(2,1)S(1)}, u32[]{:S(2)}, u32[]{:S(2)}) async-start(bf16[64,2,1024]{2,1,0:T(2,128)(2,1)} %get-tuple-element.12), calls=%async_computation.3 | async-start | bytes 524288 | tf_op jit(solution)/shard_map/all_to_all | solution.py:85
  61.7 10.1 %all-to-all-done.3 = bf16[64,2,1024]{2,1,0:T(2,128)(2,1)S(1)} async-done(((bf16[64,2,1024]{2,1,0:T(2,128)(2,1)}), bf16[64,2,1024]{2,1,0:T(2,128)(2,1)S(1)}, u32[]{:S(2)}, u32[]{:S(2)}) %all-to-all-start.3) | async-done | bytes 262176 | tf_op jit(solution)/shard_map/all_to_all | solution.py:85
  71.9 1.8 broadcast_select_fusion.2
  74.7 1.6 gather_fusion
  76.3 1.7 fusion.1
  79.1 1.3 broadcast_select_fusion.4
  80.4 1.6 gather_fusion.1
  82.0 1.6 fusion
  84.7 3.4 convolution_multiply_fusion
  89.5 5.9 %all-to-all-start = ((s32[64,1,2]{2,1,0:T(1,128)}), s32[64,1,2]{2,1,0:T(1,128)S(1)}, u32[]{:S(2)}, u32[]{:S(2)}) async-start(s32[64,1,2]{2,1,0:T(1,128)} %copy.26), calls=%async_computation | async-start | bytes 65536 | tf_op jit(solution)/shard_map/all_to_all | solution.py:100
  96.2 7.0 %all-to-all-done = s32[64,1,2]{2,1,0:T(1,128)S(1)} async-done(((s32[64,1,2]{2,1,0:T(1,128)}), s32[64,1,2]{2,1,0:T(1,128)S(1)}, u32[]{:S(2)}, u32[]{:S(2)}) %all-to-all-start) | async-done | bytes 544 | tf_op jit(solution)/shard_map/all_to_all | solution.py:100
  103.2 6.3 %all-to-all-start.1 = ((bf16[64,2,1024]{2,1,0:T(2,128)(2,1)}), bf16[64,2,1024]{2,1,0:T(2,128)(2,1)S(1)}, u32[]{:S(2)}, u32[]{:S(2)}) async-start(bf16[64,2,1024]{2,1,0:T(2,128)(2,1)} %reshape_squeeze.3), calls=%async_computation.1 | async-start | bytes 524288 | tf_op jit(solution)/shard_map/all_to_all | solution.py:93
  110.3 11.2 %all-to-all-done.1 = bf16[64,2,1024]{2,1,0:T(2,128)(2,1)S(1)} async-done(((bf16[64,2,1024]{2,1,0:T(2,128)(2,1)}), bf16[64,2,1024]{2,1,0:T(2,128)(2,1)S(1)}, u32[]{:S(2)}, u32[]{:S(2)}) %all-to-all-start.1) | async-done | bytes 262176 | tf_op jit(solution)/shard_map/all_to_all | solution.py:93
  121.5 5.9 %all-to-all-start.4 = ((bf16[64,2,1024]{2,1,0:T(2,128)(2,1)}), bf16[64,2,1024]{2,1,0:T(2,128)(2,1)S(1)}, u32[]{:S(2)}, u32[]{:S(2)}) async-start(bf16[64,2,1024]{2,1,0:T(2,128)(2,1)} %reshape.192), calls=%async_computation.4 | async-start | bytes 524288 | tf_op jit(solution)/shard_map/all_to_all | solution.py:93
  130.3 9.1 %all-to-all-done.4 = bf16[64,2,1024]{2,1,0:T(2,128)(2,1)S(1)} async-done(((bf16[64,2,1024]{2,1,0:T(2,128)(2,1)}), bf16[64,2,1024]{2,1,0:T(2,128)(2,1)S(1)}, u32[]{:S(2)}, u32[]{:S(2)}) %all-to-all-start.4) | async-done | bytes 262176 | tf_op jit(solution)/shard_map/all_to_all | solution.py:93
  140.8 105.7 %reduce-scatter.2.cloned.1.call-done = f32[16,1024]{1,0:T(8,128)} async-done(((f32[1024,1024]{1,0:T(8,128)}), f32[16,1024]{1,0:T(8,128)}) %reduce-scatter.2.cloned.1.call-update) | async-done | bytes 65552 | tf_op jit(solution)/shard_map/reduce_scatter | solution.py:140
  247.3 111.5 %all-reduce.2.cloned.1.call-done = f32[16,1024]{1,0:T(8,128)} async-done(((f32[16,1024]{1,0:T(8,128)}), f32[16,1024]{1,0:T(8,128)}) %all-reduce.2.cloned.1.call-update) | async-done | bytes 65552 | tf_op jit(solution)/shard_map/psum | solution.py:149
  358.8 1.5 copy.39
  (65 shorter events, 17.6 us)
Async XLA Ops:
  7.2 77.5 %copy-start = (bf16[1024,1024]{1,0:T(8,128)(2,1)S(1)}, bf16[1024,1024]{1,0:T(8,128)(2,1)}, u32[]{:S(2)}) copy-start(bf16[1024,1024]{1,0:T(8,128)(2,1)} %param.24) | copy-start | bytes 6291460
  8.7 21.4 %all-to-all-start.2 = ((s32[64,1,2]{2,1,0:T(1,128)}), s32[64,1,2]{2,1,0:T(1,128)S(1)}, u32[]{:S(2)}, u32[]{:S(2)}) async-start(s32[64,1,2]{2,1,0:T(1,128)} %copy.27), calls=%async_computation.2 | async-start | bytes 65536 | tf_op jit(solution)/shard_map/all_to_all | solution.py:82
  31.6 10.3 %copy-start.7 = (s32[1,1,2,4]{3,2,1,0:T(2,128)S(1)}, s32[1,1,2,4]{3,2,1,0:T(2,128)}, u32[]{:S(2)}) copy-start(s32[1,1,2,4]{3,2,1,0:T(2,128)} %param.21) | copy-start | bytes 100
  31.6 10.4 %copy-start.6 = (s32[1,1,64]{2,1,0:T(1,128)S(1)}, s32[1,1,64]{2,1,0:T(1,128)}, u32[]{:S(2)}) copy-start(s32[1,1,64]{2,1,0:T(1,128)} %param.18) | copy-start | bytes 772
  31.6 28.3 %copy-start.9 = (s32[1,1,64]{2,1,0:T(1,128)S(1)}, s32[1,1,64]{2,1,0:T(1,128)}, u32[]{:S(2)}) copy-start(s32[1,1,64]{2,1,0:T(1,128)} %param.20) | copy-start | bytes 772
  31.6 28.5 %copy-start.1 = (bf16[1,1,128,1024]{3,2,1,0:T(8,128)(2,1)S(1)}, bf16[1,1,128,1024]{3,2,1,0:T(8,128)(2,1)}, u32[]{:S(2)}) copy-start(bf16[1,1,128,1024]{3,2,1,0:T(8,128)(2,1)} %param.14) | copy-start | bytes 786436
  35.6 18.3 %all-to-all-start.5 = ((bf16[64,2,1024]{2,1,0:T(2,128)(2,1)}), bf16[64,2,1024]{2,1,0:T(2,128)(2,1)S(1)}, u32[]{:S(2)}, u32[]{:S(2)}) async-start(bf16[64,2,1024]{2,1,0:T(2,128)(2,1)} %get-tuple-element.11), calls=%async_computation.5 | async-start | bytes 524288 | tf_op jit(solution)/shard_map/all_to_all | solution.py:85
  53.9 17.9 %all-to-all-start.3 = ((bf16[64,2,1024]{2,1,0:T(2,128)(2,1)}), bf16[64,2,1024]{2,1,0:T(2,128)(2,1)S(1)}, u32[]{:S(2)}, u32[]{:S(2)}) async-start(bf16[64,2,1024]{2,1,0:T(2,128)(2,1)} %get-tuple-element.12), calls=%async_computation.3 | async-start | bytes 524288 | tf_op jit(solution)/shard_map/all_to_all | solution.py:85
  59.8 186.6 %reduce-scatter.2.cloned.1.call-start = ((), (), s32[]{:S(2)}) async-start(), calls=%async_computation.7 | async-start | bytes 4259840 | tf_op jit(solution)/shard_map/reduce_scatter | solution.py:140
  71.9 4.4 %copy-start.3 = (bf16[1,1,2,4,64,64]{5,4,3,2,1,0:T(8,128)(2,1)S(1)}, bf16[1,1,2,4,64,64]{5,4,3,2,1,0:T(8,128)(2,1)}, u32[]{:S(2)}) copy-start(bf16[1,1,2,4,64,64]{5,4,3,2,1,0:T(8,128)(2,1)} %param.22) | copy-start | bytes 196612
  76.3 2.8 copy-start.10
  79.1 1.3 copy-start.2
  82.0 2.7 copy-start.4
  88.1 0.7 copy-start.8
  88.1 21.4 %copy-start.5 = (bf16[128,1024]{1,0:T(8,128)(2,1)S(1)}, bf16[128,1024]{1,0:T(8,128)(2,1)}, u32[]{:S(2)}) copy-start(bf16[128,1024]{1,0:T(8,128)(2,1)} %get-tuple-element.16) | copy-start | bytes 786436
  89.5 13.7 %all-to-all-start = ((s32[64,1,2]{2,1,0:T(1,128)}), s32[64,1,2]{2,1,0:T(1,128)S(1)}, u32[]{:S(2)}, u32[]{:S(2)}) async-start(s32[64,1,2]{2,1,0:T(1,128)} %copy.26), calls=%async_computation | async-start | bytes 65536 | tf_op jit(solution)/shard_map/all_to_all | solution.py:100
  103.2 18.3 %all-to-all-start.1 = ((bf16[64,2,1024]{2,1,0:T(2,128)(2,1)}), bf16[64,2,1024]{2,1,0:T(2,128)(2,1)S(1)}, u32[]{:S(2)}, u32[]{:S(2)}) async-start(bf16[64,2,1024]{2,1,0:T(2,128)(2,1)} %reshape_squeeze.3), calls=%async_computation.1 | async-start | bytes 524288 | tf_op jit(solution)/shard_map/all_to_all | solution.py:93
  121.5 17.9 %all-to-all-start.4 = ((bf16[64,2,1024]{2,1,0:T(2,128)(2,1)}), bf16[64,2,1024]{2,1,0:T(2,128)(2,1)S(1)}, u32[]{:S(2)}, u32[]{:S(2)}) async-start(bf16[64,2,1024]{2,1,0:T(2,128)(2,1)} %reshape.192), calls=%async_computation.4 | async-start | bytes 524288 | tf_op jit(solution)/shard_map/all_to_all | solution.py:93
  127.4 231.4 %all-reduce.2.cloned.1.call-start = ((), (), s32[]{:S(2)}) async-start(), calls=%async_computation.8 | async-start | bytes 131072 | tf_op jit(solution)/shard_map/psum | solution.py:149
Sparse Core Ops, SparseCore 0:
  88.2 158.2 reduce-scatter.1
  248.9 109.8 all-reduce.1
where the time goes:
time: 368 us; the launch traced here: 367 us
  waiting for transfers between devices  273 us (74%)
  starting transfers between devices  43.9 us (12%)
  local copies, waits for them, and re-layouts  18.1 us (5%)
  between operations  14.3 us (4%)
  other arithmetic  9.74 us (3%)
  matrix products  7.97 us (2%)
    psum x1, waiting for transfers between devices, per_device(): gradient = lax.psum(partial_sum, 'grp')  111 us
    reduce_scatter x1, waiting for transfers between devices, per_device(): lax.psum_scatter(factor * lax.dot_general(left_rows, right_rows, (((0,),...  106 us
    all_to_all x2, waiting for transfers between devices, fetch_layer(): lax.all_to_all(found, 'store', split_axis=0, concat_axis=0, tiled=True)  21.8 us
    all_to_all x2, waiting for transfers between devices, push_layer(): lax.all_to_all(layer_rows.reshape(store_count, per_owner, features), 'sto...  20.3 us
    all_to_all x1, starting transfers between devices, fetch_layer(): lax.all_to_all(halo_wanted, 'store', split_axis=0, concat_axis=0, tiled=T...  13.5 us
    all_to_all x2, starting transfers between devices, fetch_layer(): lax.all_to_all(found, 'store', split_axis=0, concat_axis=0, tiled=True)  12.2 us
    all_to_all x2, starting transfers between devices, push_layer(): lax.all_to_all(layer_rows.reshape(store_count, per_owner, features), 'sto...  12.2 us
  transfers between devices with their start and end apart: 8, of which 8 were waited for; matrix products, arithmetic and copies ran while one was open for 3% of the time, Pallas kernels for 0%

commit v1 on v0

v1 whole, which is shorter than its diff:
```python
import functools
import math

import jax
import jax.numpy as jnp
from jax import lax
from jax.experimental import pallas as pl
from jax.experimental.pallas import tpu as pltpu
from jax.sharding import PartitionSpec as P

ALPHA = 0.1
BETA_ONE = math.log(1.5)
BETA_TWO = math.log(1.25)
GELU_K = math.sqrt(2.0 / math.pi)
GELU_C = 0.044715
MESH = pl.DeviceIdType.MESH
NX = 4
CW = 256
PW = 128
VMEM_BYTES = 63 << 20
F32 = jnp.float32
BF = jnp.bfloat16
I32 = jnp.int32


def kernel(
    dims,
    x_hbm,
    init_hbm,
    hist_hbm,
    bid_hbm,
    bcnt_hbm,
    hid_hbm,
    hcnt_hbm,
    cols_hbm,
    vals_hbm,
    w1_hbm,
    w2_hbm,
    cot_hbm,
    newhist,
    grad,
    x_v,
    init_v,
    hist_v,
    bid_v,
    bcnt_v,
    hid_v,
    hcnt_v,
    cols_v,
    vals_v,
    w1_v,
    w2_v,
    cot_v,
    id_s,
    id_r,
    stage_a,
    stage_b,
    stage_c,
    halo_s0,
    halo_s1,
    halo_r0,
    halo_r1,
    push_s0,
    push_s1,
    push_r0,
    push_r1,
    adj,
    rows1,
    rows2,
    sup,
    sup_c,
    s_full,
    g_full,
    xs,
    xr,
    ys,
    yr,
    zs,
    zr,
    zo,
    lsem,
    id_sem,
    halo_sem,
    push_sem,
    core_sem,
    x_ssem,
    x_rsem,
    y_ssem,
    y_rsem,
    z_sem,
):
    ns, nz, ny, nx, h, j = dims
    cb = h // 128
    nr = 2 * ns
    nch = h // CW
    npiece = h // PW
    me = lax.axis_index("store")
    z = lax.axis_index("grp")
    core = me % 2
    my_x = (me // 2) % nx
    my_y = me // (2 * nx)

    def device(y, x, c):
        return {"store": (y * nx + x) * 2 + c}

    locals_ = [
        (hid_hbm.at[0, 0], hid_v),
        (bid_hbm.at[0, 0], bid_v),
        (bcnt_hbm.at[0], bcnt_v),
        (hcnt_hbm.at[0], hcnt_v),
        (cols_hbm.at[0, 0], cols_v),
        (vals_hbm.at[0, 0], vals_v),
        (x_hbm.at[0, 0], x_v),
        (hist_hbm.at[:, 0], hist_v),
        (init_hbm.at[0, 0], init_v),
        (w1_hbm, w1_v),
        (w2_hbm, w2_v),
        (cot_hbm.at[0, 0], cot_v),
    ]
    loads = [pltpu.make_async_copy(a, b, lsem.at[i]) for i, (a, b) in enumerate(locals_)]
    for load in loads:
        load.start()

    barrier = pltpu.get_barrier_semaphore()

    def greet_store(i, carry):
        pl.semaphore_signal(barrier, inc=1, device_id={"store": (me + i) % ns}, device_id_type=MESH)
        return carry

    def greet_grp(i, carry):
        pl.semaphore_signal(barrier, inc=1, device_id={"grp": (z + i) % nz}, device_id_type=MESH)
        return carry

    lax.fori_loop(1, ns, greet_store, 0)
    lax.fori_loop(1, nz, greet_grp, 0)

    for i in range(6):
        loads[i].wait()
    lane_s = lax.broadcasted_iota(I32, (ns, 128), 1)
    eye_o = lax.broadcasted_iota(I32, (ns, ns), 0) == lax.broadcasted_iota(I32, (ns, ns), 1)

    def column(row):
        spread = jnp.broadcast_to(row.astype(F32), (ns, ns))
        return jnp.sum(jnp.where(eye_o, spread, 0.0), axis=1, keepdims=True)

    count_row = bcnt_v[...]
    entries = [column(hid_v[c : c + 1, :]) for c in range(2)]
    entries += [column(jnp.where(count_row > c, bid_v[c : c + 1, :], nr)) for c in range(2)]
    message = entries[3]
    for c in (2, 1, 0):
        message = jnp.where(lane_s == c, entries[c], message)
    id_s[...] = message.astype(I32).reshape(ns, 1, 128)

    slot_row = lax.broadcasted_iota(I32, (nr, ns), 0)
    owner_lane = lax.broadcasted_iota(I32, (nr, ns), 1)
    of_owner = (slot_row >> 1) == owner_lane
    slot_c = (lax.broadcasted_iota(I32, (nr, 1), 0) & 1).astype(F32)

    def live(counts):
        spread = jnp.broadcast_to(counts[...].astype(F32), (nr, ns))
        count = jnp.sum(jnp.where(of_owner, spread, 0.0), axis=1, keepdims=True)
        return jnp.where(slot_c < count, 1.0, 0.0)

    live_b = live(bcnt_v)
    live_h = live(hcnt_v)

    blk = nr // 2
    for r in range(2):
        acc = jnp.zeros((blk, 4 * blk), F32)
        for k in range(4):
            lane = lax.broadcasted_iota(I32, (blk, 4 * blk), 1)
            row = lax.broadcasted_iota(I32, (blk, 4 * blk), 0)
            target = row + cols_v[r : r + 1, k : k + 1] * blk
            select = jnp.where(lane == target, 1.0, 0.0).astype(BF)
            acc += jnp.dot(vals_v[r, k], select, preferred_element_type=F32)
        adj[r * blk : (r + 1) * blk, :] = acc.astype(BF)

    def to_message(rows, stage, buffer):
        for b in range(cb):
            stage[pl.ds(b, nr, stride=cb), :] = rows[:, b * 128 : (b + 1) * 128].astype(F32)
        buffer[...] = stage[...].astype(BF).reshape(ns, 2 * cb, 128)

    loads[6].wait()
    to_message(x_v[...], stage_a, push_s0)
    rows1[0:nr, :] = (x_v[...].astype(F32) * live_b).astype(BF)
    loads[7].wait()

    pl.semaphore_wait(barrier, ns - 1 + nz - 1)

    def exchange(source, target, ssem, rsem):
        def send(i, carry):
            peer = (me + i) % ns
            pltpu.make_async_remote_copy(
                src_ref=source.at[peer],
                dst_ref=target.at[me],
                send_sem=ssem,
                recv_sem=rsem,
                device_id={"store": peer},
                device_id_type=MESH,
            ).start()
            return carry

        lax.fori_loop(1, ns, send, 0)

    def arrive(buffer, count, sem):
        part = buffer.at[pl.ds(0, count)]
        pltpu.make_async_copy(part, part, sem).wait()

    exchange(id_s, id_r, id_sem.at[0], id_sem.at[1])
    exchange(push_s0, push_r0, push_sem.at[0], push_sem.at[1])
    id_r[me] = id_s[me]
    push_r0[me] = push_s0[me]
    arrive(id_r, ns - 1, id_sem.at[1])

    asked = id_r[...].reshape(ns, 128)
    lane_r = lax.broadcasted_iota(I32, (ns, nr), 1)

    def hot(k):
        return jnp.where(asked[:, k : k + 1] == lane_r, 1.0, 0.0)

    wanted = jnp.concatenate([hot(0), hot(1)], axis=0).astype(BF)

    def gather(layer, stage, buffer):
        found = jnp.dot(wanted, hist_v[layer], preferred_element_type=F32)
        for c in range(2):
            for b in range(cb):
                stage[pl.ds(c * cb + b, ns, stride=2 * cb), :] = found[
                    c * ns : (c + 1) * ns, b * 128 : (b + 1) * 128
                ]
        buffer[...] = stage[...].astype(BF).reshape(ns, 2 * cb, 128)

    gather(0, stage_b, halo_s0)
    exchange(halo_s0, halo_r0, halo_sem.at[0], halo_sem.at[1])
    gather(1, stage_c, halo_s1)
    exchange(halo_s1, halo_r1, halo_sem.at[2], halo_sem.at[3])
    halo_r0[me] = halo_s0[me]
    halo_r1[me] = halo_s1[me]

    def land(buffer, stage, rows):
        stage[...] = buffer[...].reshape(nr * cb, 128).astype(F32)
        for b in range(cb):
            block = stage[pl.ds(b, nr, stride=cb), :] * live_h
            rows[nr : 2 * nr, b * 128 : (b + 1) * 128] = block.astype(BF)

    def support(rows):
        for n in range(nch):
            part = slice(n * CW, (n + 1) * CW)
            aggregate = jnp.dot(adj[...], rows[:, part], preferred_element_type=F32)
            mixed = (1.0 - ALPHA) * aggregate + ALPHA * init_v[:, part].astype(F32)
            sup[:, part] = mixed.astype(BF)

    def preact(weight, beta, n):
        part = slice(n * CW, (n + 1) * CW)
        product = jnp.dot(sup[...], weight[:, part], preferred_element_type=F32)
        return (1.0 - beta) * sup[:, part].astype(F32) + beta * product

    loads[8].wait()
    loads[9].wait()
    arrive(halo_r0, ns - 1, halo_sem.at[1])
    land(halo_r0, stage_b, rows1)
    support(rows1)
    for n in range(nch):
        part = slice(n * CW, (n + 1) * CW)
        pre = preact(w1_v, BETA_ONE, n)
        inner = jnp.tanh(GELU_K * (pre + GELU_C * (pre * pre * pre)))
        fresh = (0.5 * pre * (1.0 + inner)).astype(BF).astype(F32)
        rows2[0:nr, part] = (fresh * live_b).astype(BF)
        for b in range(CW // 128):
            stage_a[pl.ds(n * (CW // 128) + b, nr, stride=cb), :] = fresh[:, b * 128 : (b + 1) * 128]
    push_s1[...] = stage_a[...].astype(BF).reshape(ns, 2 * cb, 128)
    exchange(push_s1, push_r1, push_sem.at[2], push_sem.at[3])
    push_r1[me] = push_s1[me]

    loads[10].wait()
    loads[11].wait()
    arrive(halo_r1, ns - 1, halo_sem.at[3])
    land(halo_r1, stage_c, rows2)
    support(rows2)

    wide = 4 * nx * j
    half = wide // 2
    lane_to = lax.broadcasted_iota(I32, (wide, wide), 1)
    lane_from = lax.broadcasted_iota(I32, (wide, wide), 0)
    lg_j = j.bit_length() - 1
    lg_x = nx.bit_length() - 1
    from_j = lane_from & (j - 1)
    from_c = (lane_from >> lg_j) & 1
    from_x = (lane_from >> (lg_j + 1)) & (nx - 1)
    from_y = lane_from >> (lg_j + 1 + lg_x)
    goes = from_c * half + from_y * (nx * j) + from_x * j + from_j
    shuffle = jnp.where(goes == lane_to, 1.0, 0.0).astype(BF)
    for t in range(h // wide):
        moved = jnp.dot(sup[:, t * wide : (t + 1) * wide], shuffle, preferred_element_type=F32).astype(BF)
        sup_c[0, :, t * half : (t + 1) * half] = moved[:, :half]
        sup_c[1, :, t * half : (t + 1) * half] = moved[:, half:]
    partner = device(my_y, my_x, 1 - core)
    send_s = pltpu.make_async_remote_copy(
        src_ref=sup_c.at[1 - core],
        dst_ref=s_full.at[pl.ds(nr, nr)],
        send_sem=core_sem.at[0],
        recv_sem=core_sem.at[1],
        device_id=partner,
        device_id_type=MESH,
    )
    send_s.start()
    s_full[0:nr, :] = sup_c[core]
    for n in range(nch):
        part = slice(n * CW, (n + 1) * CW)
        pre = preact(w2_v, BETA_TWO, n)
        square = pre * pre
        inner = jnp.tanh(GELU_K * (pre + GELU_C * (square * pre)))
        slope = 0.5 * (1.0 + inner) + 0.5 * pre * (1.0 - inner * inner) * (
            GELU_K * (1.0 + 3.0 * GELU_C * square)
        )
        g_full[0:nr, part] = (live_b * (cot_v[:, part].astype(F32) * slope)).astype(BF)
    send_g = pltpu.make_async_remote_copy(
        src_ref=g_full.at[pl.ds(0, nr)],
        dst_ref=g_full.at[pl.ds(nr, nr)],
        send_sem=core_sem.at[2],
        recv_sem=core_sem.at[3],
        device_id=partner,
        device_id_type=MESH,
    )
    send_g.start()
    send_s.wait()
    send_g.wait()

    factor = BETA_TWO / math.sqrt(nz * ns * nr)
    for k in range(nch):
        share = factor * lax.dot_general(
            s_full[...],
            g_full[:, k * CW : (k + 1) * CW],
            (((0,), (0,)), ((), ())),
            preferred_element_type=F32,
        )
        for y in range(ny):
            for x in range(nx):
                at = (y * nx + x) * j
                xs[k, x, y * j : (y + 1) * j, :] = share[at : at + j, :].astype(BF)
        for i in range(1, nx):
            to_x = (my_x + i) % nx
            pltpu.make_async_remote_copy(
                src_ref=xs.at[k, to_x],
                dst_ref=xr.at[k, i - 1],
                send_sem=x_ssem.at[k],
                recv_sem=x_rsem.at[k],
                device_id=device(my_y, to_x, core),
                device_id_type=MESH,
            ).start()

    eye_r = lax.broadcasted_iota(I32, (nr, nr), 0) == lax.broadcasted_iota(I32, (nr, nr), 1)
    placed = jnp.concatenate([hot(2), hot(3)], axis=0)
    kept = jnp.where(eye_r, 1.0 - jnp.sum(placed, axis=0, keepdims=True), 0.0)
    place = jnp.concatenate([placed, kept], axis=0).astype(BF)

    def write_layer(layer, buffer, stage, rows):
        stage[...] = buffer[...].reshape(nr * cb, 128).astype(F32)
        for c in range(2):
            for b in range(cb):
                rows[c * ns : (c + 1) * ns, b * 128 : (b + 1) * 128] = stage[
                    pl.ds(c * cb + b, ns, stride=2 * cb), :
                ].astype(BF)
        rows[nr : 2 * nr, :] = hist_v[layer]
        newhist[layer, 0] = lax.dot_general(
            place, rows[...], (((0,), (0,)), ((), ())), preferred_element_type=F32
        ).astype(BF)

    arrive(push_r0, ns - 1, push_sem.at[1])
    write_layer(0, push_r0, stage_b, rows1)

    for k in range(nch):
        arrive(xr.at[k], nx - 1, x_rsem.at[k])
        total = xs[k, my_x].astype(F32)
        for i in range(nx - 1):
            total += xr[k, i].astype(F32)
        ys[k] = total.astype(BF).reshape(ny, j, CW)
        for i in range(1, ny):
            to_y = (my_y + i) % ny
            pltpu.make_async_remote_copy(
                src_ref=ys.at[k, to_y],
                dst_ref=yr.at[k, i - 1],
                send_sem=y_ssem.at[k],
                recv_sem=y_rsem.at[k],
                device_id=device(to_y, my_x, core),
                device_id_type=MESH,
            ).start()

    arrive(push_r1, ns - 1, push_sem.at[3])
    write_layer(1, push_r1, stage_c, rows2)

    per = CW // PW
    for k in range(nch):
        arrive(yr.at[k], ny - 1, y_rsem.at[k])
        total = ys[k, my_y].astype(F32)
        for i in range(ny - 1):
            total += yr[k, i].astype(F32)
        for p in range(per):
            piece = k * per + p
            goal = piece % nz
            zs[piece] = total[:, p * PW : (p + 1) * PW].astype(BF)

            @pl.when(z != goal)
            def _():
                pltpu.make_async_remote_copy(
                    src_ref=zs.at[piece],
                    dst_ref=zr.at[z],
                    send_sem=z_sem.at[0],
                    recv_sem=z_sem.at[1],
                    device_id={"grp": goal},
                    device_id_type=MESH,
                ).start()

            @pl.when(z == goal)
            def _():
                zr[z] = zs[piece]

    @pl.when(z < npiece)
    def _():
        arrive(zr, nz - 1, z_sem.at[1])
        total = zr[0].astype(F32)
        for i in range(1, nz):
            total += zr[i].astype(F32)
        zo[z] = total

        def send(i, carry):
            pltpu.make_async_remote_copy(
                src_ref=zo.at[z],
                dst_ref=zo.at[z],
                send_sem=z_sem.at[2],
                recv_sem=z_sem.at[3],
                device_id={"grp": (z + i) % nz},
                device_id_type=MESH,
            ).start()
            return carry

        lax.fori_loop(1, nz, send, 0)
        arrive(zo, npiece - 1, z_sem.at[3])

    @pl.when(z >= npiece)
    def _():
        arrive(zo, npiece, z_sem.at[3])

    for p in range(npiece):
        grad[:, p * PW : (p + 1) * PW] = zo[p]

    arrive(id_s, ns - 1, id_sem.at[0])
    arrive(push_s0, ns - 1, push_sem.at[0])
    arrive(push_s1, ns - 1, push_sem.at[2])
    arrive(halo_s0, ns - 1, halo_sem.at[0])
    arrive(halo_s1, ns - 1, halo_sem.at[2])
    for k in range(nch):
        arrive(xs.at[k], nx - 1, x_ssem.at[k])
        arrive(ys.at[k], ny - 1, y_ssem.at[k])

    @pl.when(z < npiece)
    def _():
        arrive(zs, npiece - 1, z_sem.at[0])
        arrive(zo, nz - 1, z_sem.at[2])

    @pl.when(z >= npiece)
    def _():
        arrive(zs, npiece, z_sem.at[0])


def per_device(*args):
    x, init, hist, bid, bcnt, hid, hcnt, cols, vals, w1, w2, cot = args
    ns, nz = lax.axis_size("store"), lax.axis_size("grp")
    h = x.shape[-1]
    nx = NX
    ny = ns // (2 * nx)
    j = h // ns
    nr = 2 * ns
    blk = nr // 2
    cb = h // 128
    nch = h // CW
    npiece = h // PW
    vm = pltpu.VMEM
    dma = pltpu.SemaphoreType.DMA
    slots = vm((ns, 2 * cb, 128), BF)
    stage = vm((nr * cb, 128), F32)
    scratch = [
        vm((nr, h), BF),
        vm((nr, h), BF),
        vm((2, nr, h), BF),
        vm((2, ns), I32),
        vm((1, ns), I32),
        vm((2, ns), I32),
        vm((1, ns), I32),
        vm((2, 4), I32),
        vm((2, 4, blk, blk), BF),
        vm((h, h), BF),
        vm((h, h), BF),
        vm((nr, h), BF),
        vm((ns, 1, 128), I32),
        vm((ns, 1, 128), I32),
        stage,
        stage,
        stage,
        slots,
        slots,
        slots,
        slots,
        slots,
        slots,
        slots,
        slots,
        vm((nr, 2 * nr), BF),
        vm((2 * nr, h), BF),
        vm((2 * nr, h), BF),
        vm((nr, h), BF),
        vm((2, nr, h // 2), BF),
        vm((2 * nr, h // 2), BF),
        vm((2 * nr, h), BF),
        vm((nch, nx, ny * j, CW), BF),
        vm((nch, nx - 1, ny * j, CW), BF),
        vm((nch, ny, j, CW), BF),
        vm((nch, ny - 1, j, CW), BF),
        vm((npiece, j, PW), BF),
        vm((nz, j, PW), BF),
        vm((nz, j, PW), F32),
        dma((12,)),
        dma((2,)),
        dma((4,)),
        dma((4,)),
        dma((4,)),
        dma((nch,)),
        dma((nch,)),
        dma((nch,)),
        dma((nch,)),
        dma((4,)),
    ]
    return pl.pallas_call(
        functools.partial(kernel, (ns, nz, ny, nx, h, j)),
        out_shape=(
            jax.ShapeDtypeStruct((2, 1, nr, h), BF),
            jax.ShapeDtypeStruct((j, h), F32),
        ),
        in_specs=[pl.BlockSpec(memory_space=pl.ANY)] * 12,
        out_specs=(
            pl.BlockSpec(memory_space=pltpu.VMEM),
            pl.BlockSpec(memory_space=pltpu.VMEM),
        ),
        scratch_shapes=scratch,
        compiler_params=pltpu.CompilerParams(
            collective_id=0, has_side_effects=True, vmem_limit_bytes=VMEM_BYTES
        ),
        name="gcnii",
    )(
        x,
        init,
        hist,
        jnp.swapaxes(bid, 2, 3),
        bcnt,
        jnp.swapaxes(hid, 2, 3),
        hcnt,
        cols,
        vals,
        w1,
        w2,
        cot,
    )


def solution(mesh):
    in_specs = (
        P("grp", "store", None, None),
        P("grp", "store", None, None),
        P(None, "grp", "store", None),
        P("grp", "store", None, None),
        P("grp", "store", None),
        P("grp", "store", None, None),
        P("grp", "store", None),
        P("grp", "store", None, None),
        P("grp", "store", None, None, None, None),
        P(),
        P(),
        P("grp", "store", None, None),
    )
    out_specs = (P(None, "grp", "store", None), P("store", None))
    return jax.shard_map(
        per_device, mesh=mesh, in_specs=in_specs, out_specs=out_specs, check_vma=False
    )
```

time: 368 us -> 81.5 us (0.22)
  waiting for transfers between devices: 273 us -> 0 us
  Pallas kernels: 0 us -> 76.8 us
  starting transfers between devices: 43.9 us -> 0 us
  local copies, waits for them, and re-layouts: 18.1 us -> 3.34 us
  between operations: 14.3 us -> 0.64 us
  other arithmetic: 9.74 us -> 0 us
  matrix products: 7.97 us -> 0 us
    psum x1 -> x0, waiting for transfers between devices: 111 us -> none  [per_device(): gradient = lax.psum(partial_sum, 'grp')]
    reduce_scatter x1 -> x0, waiting for transfers between devices: 106 us -> none  [per_device(): lax.psum_scatter(factor * lax.dot_general(left_rows, right_rows, (((0,),...]
    pallas_call x0 -> x1, Pallas kernels: none -> 76.8 us  [per_device(): pl.pallas_call(functools.partial(kernel, (ns, nz, ny, nx, h, j)), out_sha...]
    all_to_all x6 -> x0, waiting for transfers between devices: 55.9 us -> none  [the longest x2 21.8 us: fetch_layer(): lax.all_to_all(found, 'store', split_axis=0, concat_axis=0, tiled=True)]
    all_to_all x6 -> x0, starting transfers between devices: 43.8 us -> none  [the longest x1 13.5 us: fetch_layer(): lax.all_to_all(halo_wanted, 'store', split_axis=0, concat_axis=0, tiled=T...]
    dot_general x4 -> x0, matrix products: 7.97 us -> none  [the longest x1 3.35 us: per_device(): lax.dot_general(left_rows, right_rows, (((0,), (0,)), ((), ())), preferre...]
    gather x6 -> x0, local copies, waits for them, and re-layouts: 5.84 us -> none  [the longest x2 3.21 us: spread(): picked = blocks[col_blocks]]
    select_n x7 -> x0, other arithmetic: 4.9 us -> none  [the longest x2 2.3 us: fetch_layer(): jnp.take(history_shard[which_layer], lax.all_to_all(halo_wanted, 'store',...]
  transfers between devices with their start and end apart: 8 -> 0, of which waited for: 8 -> 0; matrix products, arithmetic and copies ran while one was open for 3% -> 0% of each run, Pallas kernels for 0% -> 0%
where the time goes in v1:
time: 81.5 us; the launch traced here: 80.8 us
  Pallas kernels  76.8 us (94%)
  local copies, waits for them, and re-layouts  3.34 us (4%)
    pallas_call x1, Pallas kernels, per_device(): pl.pallas_call(functools.partial(kernel, (ns, nz, ny, nx, h, j)), out_sha...  76.8 us
    unnamed x2, local copies, waits for them, and re-layouts  3.34 us

profile of v1, /device:TPU:6, one launch (start us, length us, event | category | flops | bytes accessed | tf_op | source)
XLA Modules:
  0.0 80.8 jit_solution(1279884585825776082)
XLA Ops:
  0.6 76.8 %gcnii.1 = (bf16[2,1,128,1024]{3,2,1,0:T(8,128)(2,1)}, f32[16,1024]{1,0:T(8,128)}) custom-call(bf16[1,1,128,1024]{3,2,1,0:T(8,128)(2,1)} %x_hbm.1, bf16[1,1,128,1024]{3,2,1,0:T(8,128)(2,1)} %init_hbm.1, bf16[2,1,128,1024]{3,2,1,0:T(8,128)(2,1)} %hist_hbm.1, s32[1,1,2,64]{3,2,1,0:T(2,128)} %bitcast.2, s32[1,1,64]{2,1,0:T(1,128)} %bcnt_hbm.1, ...), custom_call_target="tpu_custom_call" | custom-call | tf_op jit(solution)/shard_map/gcnii/pallas_call | solution.py:532
  77.4 1.9 %copy.16 = bf16[2,1,128,1024]{3,2,1,0:T(8,128)(2,1)} copy(bf16[2,1,128,1024]{3,2,1,0:T(8,128)(2,1)} %get-tuple-element.4) | data formatting | bytes 1048576
  79.3 1.5 %copy.17 = f32[16,1024]{1,0:T(8,128)} copy(f32[16,1024]{1,0:T(8,128)} %get-tuple-element.5) | data formatting | bytes 131072

commit v2 on v1

v2 whole, which is shorter than its diff:
```python
import functools
import math

import jax
import jax.numpy as jnp
from jax import lax
from jax.experimental import pallas as pl
from jax.experimental.pallas import tpu as pltpu
from jax.sharding import PartitionSpec as P

ALPHA = 0.1
BETA_ONE = math.log(1.5)
BETA_TWO = math.log(1.25)
GELU_K = math.sqrt(2.0 / math.pi)
GELU_C = 0.044715
MESH = pl.DeviceIdType.MESH
NX = 4
WIDTHS = (256, 256, 256, 256)
PATHS = "xxxx"
FAR_FIRST = 1
CW = 256
FAR = {8: (3, 6), 2: (1, 2)}
PUSH0 = 3
NEAR1 = 0
VMEM_BYTES = 63 << 20
F32 = jnp.float32
BF = jnp.bfloat16
I32 = jnp.int32


def kernel(
    dims,
    x_hbm,
    init_hbm,
    hist_hbm,
    bid_hbm,
    bcnt_hbm,
    hid_hbm,
    hcnt_hbm,
    cols_hbm,
    vals_hbm,
    w1_hbm,
    w2_hbm,
    cot_hbm,
    newhist,
    grad,
    x_v,
    init_v,
    hist_v,
    bid_v,
    bcnt_v,
    hid_v,
    hcnt_v,
    cols_v,
    vals_v,
    w1_v,
    w2_v,
    cot_v,
    id_s,
    id_r,
    stage_a,
    stage_b,
    stage_c,
    halo_s0,
    halo_s1,
    halo_r0,
    halo_r1,
    push_s0,
    push_s1,
    push_r0,
    push_r1,
    adj,
    rows1,
    rows2,
    sup,
    sup_c,
    s_pair,
    hist_o,
    lsem,
    id_sem,
    halo_sem,
    push_sem,
    core_sem,
    x_ssem,
    x_rsem,
    y_ssem,
    y_rsem,
    z_ssem,
    z_rsem,
    osem,
    *chunks,
):
    ns, nz, ny, nx, h, j = dims
    cb = h // 128
    nr = 2 * ns
    nch = len(WIDTHS)
    starts = [sum(WIDTHS[:k]) for k in range(nch)]
    g_pair, xs, xr, ys, yr, zr = (chunks[i * nch : (i + 1) * nch] for i in range(6))
    w = 2 * nx
    far_lo, far_hi = (d * w for d in FAR[ny])
    near = [(1, far_lo), (far_hi, ns)]
    far = [(far_lo, far_hi)]
    me = lax.axis_index("store")
    z = lax.axis_index("grp")
    core = me % 2
    my_x = (me // 2) % nx
    my_y = me // w
    my_w = me % w

    def device(y, x, c):
        return {"store": (y * nx + x) * 2 + c}

    locals_ = [
        (hid_hbm.at[0, 0], hid_v),
        (bid_hbm.at[0, 0], bid_v),
        (bcnt_hbm.at[0], bcnt_v),
        (hcnt_hbm.at[0], hcnt_v),
        (cols_hbm.at[0, 0], cols_v),
        (vals_hbm.at[0, 0], vals_v),
        (x_hbm.at[0, 0], x_v),
        (hist_hbm.at[:, 0], hist_v),
        (init_hbm.at[0, 0], init_v),
        (w1_hbm, w1_v),
        (w2_hbm, w2_v),
        (cot_hbm.at[0, 0], cot_v),
    ]
    loads = [pltpu.make_async_copy(a, b, lsem.at[i]) for i, (a, b) in enumerate(locals_)]
    owed = {}
    for i, load in enumerate(loads):
        load.start()
        owed["load", i] = load.wait

    def settle(*name):
        owed.pop(name)()

    def finish():
        for name in list(owed):
            owed.pop(name)()

    barrier = pltpu.get_barrier_semaphore()

    def greet_store(i, carry):
        pl.semaphore_signal(barrier, inc=1, device_id={"store": (me + i) % ns}, device_id_type=MESH)
        return carry

    def greet_grp(i, carry):
        pl.semaphore_signal(barrier, inc=1, device_id={"grp": (z + i) % nz}, device_id_type=MESH)
        return carry

    lax.fori_loop(1, ns, greet_store, 0)
    lax.fori_loop(1, nz, greet_grp, 0)

    for i in range(3):
        settle("load", i)
    lane_s = lax.broadcasted_iota(I32, (ns, 128), 1)
    eye_o = lax.broadcasted_iota(I32, (ns, ns), 0) == lax.broadcasted_iota(I32, (ns, ns), 1)

    def column(row):
        spread = jnp.broadcast_to(row.astype(F32), (ns, ns))
        return jnp.sum(jnp.where(eye_o, spread, 0.0), axis=1, keepdims=True)

    count_row = bcnt_v[...]
    entries = [column(hid_v[c : c + 1, :]) for c in range(2)]
    entries += [column(jnp.where(count_row > c, bid_v[c : c + 1, :], nr)) for c in range(2)]
    message = entries[3]
    for c in (2, 1, 0):
        message = jnp.where(lane_s == c, entries[c], message)
    id_s[...] = message.astype(I32).reshape(ns, 1, 128)

    pl.semaphore_wait(barrier, ns - 1 + nz - 1)

    def arrive(buffer, count, sem):
        part = buffer.at[pl.ds(0, count)]
        pltpu.make_async_copy(part, part, sem).wait()

    def send_all(ranges, source, target, ssem, rsem, by_owner):
        def send(i, carry):
            along = i // w
            column = (my_w + i % w) % w
            peer = ((my_y + along) % ny) * w + column
            here = along * w + column
            there = ((ny - along) % ny) * w + my_w
            pltpu.make_async_remote_copy(
                src_ref=source.at[here if by_owner else peer],
                dst_ref=target.at[me if by_owner else there],
                send_sem=ssem,
                recv_sem=rsem,
                device_id={"store": peer},
                device_id_type=MESH,
            ).start()
            return carry

        for low, high in ranges:
            if low < high:
                lax.fori_loop(low, high, send, 0)
        return sum(high - low for low, high in ranges)

    def owe(name, buffer, count, sem):
        owed[name] = functools.partial(arrive, buffer, count, sem)

    def push(name, source, target, sems):
        count = send_all(near + far, source, target, sems.at[0], sems.at[1], False)
        owe((name, "out"), source, count, sems.at[0])
        owe((name, "in"), target, count, sems.at[1])

    for part, ranges in enumerate((far, near)):
        count = send_all(ranges, id_s, id_r, id_sem.at[part, 0], id_sem.at[part, 1], False)
        owe(("ids", "out", part), id_s, count, id_sem.at[part, 0])
        owe(("ids", "in", part), id_r, count, id_sem.at[part, 1])
    id_r[my_w] = id_s[me]

    for i in range(3, 6):
        settle("load", i)
    slot_row = lax.broadcasted_iota(I32, (nr, ns), 0)
    owner_lane = lax.broadcasted_iota(I32, (nr, ns), 1)
    of_owner = (slot_row >> 1) == owner_lane
    slot_c = (lax.broadcasted_iota(I32, (nr, 1), 0) & 1).astype(F32)

    def live(counts):
        spread = jnp.broadcast_to(counts[...].astype(F32), (nr, ns))
        count = jnp.sum(jnp.where(of_owner, spread, 0.0), axis=1, keepdims=True)
        return jnp.where(slot_c < count, 1.0, 0.0)

    live_b = live(bcnt_v)
    live_h = live(hcnt_v)

    blk = nr // 2
    for r in range(2):
        acc = jnp.zeros((blk, 4 * blk), F32)
        for k in range(4):
            lane = lax.broadcasted_iota(I32, (blk, 4 * blk), 1)
            row = lax.broadcasted_iota(I32, (blk, 4 * blk), 0)
            target = row + cols_v[r : r + 1, k : k + 1] * blk
            select = jnp.where(lane == target, 1.0, 0.0).astype(BF)
            acc += jnp.dot(vals_v[r, k], select, preferred_element_type=F32)
        adj[r * blk : (r + 1) * blk, :] = acc.astype(BF)

    def to_message(rows, stage, buffer):
        for b in range(cb):
            stage[pl.ds(b, nr, stride=cb), :] = rows[:, b * 128 : (b + 1) * 128].astype(F32)
        buffer[...] = stage[...].astype(BF).reshape(ns, 2 * cb, 128)

    settle("load", 6)
    rows1[0:nr, :] = (x_v[...].astype(F32) * live_b).astype(BF)
    to_message(rows1[0:nr, :], stage_a, push_s0)
    if PUSH0 == 3:
        push("push0", push_s0, push_r0, push_sem.at[0])
    push_r0[my_w] = push_s0[me]
    settle("load", 7)
    def hot(k, low, high):
        asked = id_r[low:high].reshape(high - low, 128)
        lane_r = lax.broadcasted_iota(I32, (high - low, nr), 1)
        return jnp.where(asked[:, k : k + 1] == lane_r, 1.0, 0.0)

    def gather(layer, ranges, stage, buffer):
        for low, high in ranges:
            size = high - low
            if size == 0:
                continue
            wanted = jnp.concatenate([hot(0, low, high), hot(1, low, high)], axis=0).astype(BF)
            found = jnp.dot(wanted, hist_v[layer], preferred_element_type=F32)
            for c in range(2):
                for b in range(cb):
                    stage[pl.ds(low * 2 * cb + c * cb + b, size, stride=2 * cb), :] = found[
                        c * size : (c + 1) * size, b * 128 : (b + 1) * 128
                    ]
            rows = stage[low * 2 * cb : high * 2 * cb, :]
            buffer[low:high] = rows.astype(BF).reshape(size, 2 * cb, 128)

    def reply(layer, ranges, source, target, sems, part):
        count = send_all(ranges, source, target, sems.at[part], sems.at[2], True)
        owe(("reply", layer, part), source, count, sems.at[part])

    near_rows = [(0, far_lo), (far_hi, ns)]
    settle("ids", "in", 1)
    gather(0, near_rows, stage_b, halo_s0)
    reply(0, near, halo_s0, halo_r0, halo_sem.at[0], 0)
    if NEAR1 == 1:
        gather(1, near_rows, stage_c, halo_s1)
        reply(1, near, halo_s1, halo_r1, halo_sem.at[1], 0)
    settle("ids", "in", 0)
    gather(0, far, stage_b, halo_s0)
    reply(0, far, halo_s0, halo_r0, halo_sem.at[0], 1)
    gather(1, far, stage_c, halo_s1)
    reply(1, far, halo_s1, halo_r1, halo_sem.at[1], 1)
    if NEAR1 == 0:
        gather(1, near_rows, stage_c, halo_s1)
        reply(1, near, halo_s1, halo_r1, halo_sem.at[1], 0)
    owe(("halo0", "in"), halo_r0, ns - 1, halo_sem.at[0, 2])
    owe(("halo1", "in"), halo_r1, ns - 1, halo_sem.at[1, 2])
    if PUSH0 == 0:
        push("push0", push_s0, push_r0, push_sem.at[0])
    halo_r0[me] = halo_s0[my_w]
    halo_r1[me] = halo_s1[my_w]

    def land(buffer, stage, rows):
        stage[...] = buffer[...].reshape(nr * cb, 128).astype(F32)
        for b in range(cb):
            block = stage[pl.ds(b, nr, stride=cb), :] * live_h
            rows[nr : 2 * nr, b * 128 : (b + 1) * 128] = block.astype(BF)

    def support(rows):
        for n in range(h // CW):
            part = slice(n * CW, (n + 1) * CW)
            aggregate = jnp.dot(adj[...], rows[:, part], preferred_element_type=F32)
            mixed = (1.0 - ALPHA) * aggregate + ALPHA * init_v[:, part].astype(F32)
            sup[:, part] = mixed.astype(BF)

    def preact(weight, beta, part):
        product = jnp.dot(sup[...], weight[:, part], preferred_element_type=F32)
        return (1.0 - beta) * sup[:, part].astype(F32) + beta * product

    settle("load", 8)
    settle("load", 9)
    settle("halo0", "in")
    land(halo_r0, stage_b, rows1)
    support(rows1)
    for n in range(h // CW):
        part = slice(n * CW, (n + 1) * CW)
        pre = preact(w1_v, BETA_ONE, part)
        inner = jnp.tanh(GELU_K * (pre + GELU_C * (pre * pre * pre)))
        fresh = (0.5 * pre * (1.0 + inner)).astype(BF).astype(F32)
        rows2[0:nr, part] = (fresh * live_b).astype(BF)
    to_message(rows2[0:nr, :], stage_a, push_s1)
    push("push1", push_s1, push_r1, push_sem.at[1])
    push_r1[my_w] = push_s1[me]
    if PUSH0 == 1:
        push("push0", push_s0, push_r0, push_sem.at[0])

    settle("load", 10)
    settle("load", 11)
    settle("halo1", "in")
    land(halo_r1, stage_c, rows2)
    support(rows2)

    wide = 4 * nx * j
    half = wide // 2
    lane_from = lax.broadcasted_iota(I32, (wide, wide), 1)
    row_to = lax.broadcasted_iota(I32, (wide, wide), 0)
    lg_j = j.bit_length() - 1
    lg_x = nx.bit_length() - 1
    from_j = lane_from & (j - 1)
    from_c = (lane_from >> lg_j) & 1
    from_x = (lane_from >> (lg_j + 1)) & (nx - 1)
    from_y = lane_from >> (lg_j + 1 + lg_x)
    goes = from_c * half + from_y * (nx * j) + from_x * j + from_j
    shuffle = jnp.where(goes == row_to, 1.0, 0.0).astype(BF)
    for t in range(h // wide):
        moved = lax.dot_general(
            shuffle,
            sup[:, t * wide : (t + 1) * wide],
            (((1,), (1,)), ((), ())),
            preferred_element_type=F32,
        ).astype(BF)
        sup_c[0, t * half : (t + 1) * half, :] = moved[:half]
        sup_c[1, t * half : (t + 1) * half, :] = moved[half:]
    partner = device(my_y, my_x, 1 - core)

    def to_partner(name, source, target, ssem, rsem):
        copy = pltpu.make_async_remote_copy(
            src_ref=source,
            dst_ref=target,
            send_sem=ssem,
            recv_sem=rsem,
            device_id=partner,
            device_id_type=MESH,
        )
        copy.start()
        owed[name] = copy.wait

    to_partner(("core", "s"), sup_c.at[1 - core], s_pair.at[1], core_sem.at[nch, 0], core_sem.at[nch, 1])
    s_pair[0] = sup_c[core]

    factor = BETA_TWO / math.sqrt(nz * ns * nr)

    along_x = (nx, my_x, lambda to: device(my_y, to, core))
    along_y = (ny, my_y, lambda to: device(to, my_x, core))

    def steps(count):
        if FAR_FIRST:
            return sorted(range(1, count), key=lambda i: -min(i, count - i))
        return range(1, count)

    def spread(name, k, axis, source, target, ssem, rsem):
        count, mine, to_device = axis
        for i in steps(count):
            to = (mine + i) % count
            pltpu.make_async_remote_copy(
                src_ref=source.at[to],
                dst_ref=target.at[i - 1],
                send_sem=ssem,
                recv_sem=rsem,
                device_id=to_device(to),
                device_id_type=MESH,
            ).start()
        owe((name, "in", k), target, count - 1, rsem)
        owe((name, "out", k), source, count - 1, ssem)

    def summed(axis, source, target):
        total = source[axis[1]].astype(F32)
        for i in range(axis[0] - 1):
            total += target[i].astype(F32)
        return total

    for n in range(nch + 1):
        if n < nch:
            part = slice(starts[n], starts[n] + WIDTHS[n])
            pre = preact(w2_v, BETA_TWO, part)
            square = pre * pre
            inner = jnp.tanh(GELU_K * (pre + GELU_C * (square * pre)))
            slope = 0.5 * (1.0 + inner) + 0.5 * pre * (1.0 - inner * inner) * (
                GELU_K * (1.0 + 3.0 * GELU_C * square)
            )
            g_pair[n][0] = (live_b * (cot_v[:, part].astype(F32) * slope)).astype(BF)
            to_partner(("core", n), g_pair[n].at[0], g_pair[n].at[1], core_sem.at[n, 0], core_sem.at[n, 1])
        if n == 1:
            settle("core", "s")
        if n >= 1:
            k = n - 1
            settle("core", k)
            share = factor * jnp.dot(
                jnp.concatenate([s_pair[0], s_pair[1]], axis=1),
                g_pair[k][...].reshape(2 * nr, WIDTHS[k]),
                preferred_element_type=F32,
            )
            if PATHS[k] == "x":
                for y in range(ny):
                    for x in range(nx):
                        at = (y * nx + x) * j
                        xs[k][x, y * j : (y + 1) * j, :] = share[at : at + j, :].astype(BF)
            else:
                xs[k][...] = share.astype(BF).reshape(ny, nx * j, WIDTHS[k])
            first = along_x if PATHS[k] == "x" else along_y
            spread("x", k, first, xs[k], xr[k], x_ssem.at[k], x_rsem.at[k])

    for k in range(nch + 1):
        if k < nch:
            first, second = (along_x, along_y) if PATHS[k] == "x" else (along_y, along_x)
            settle("x", "in", k)
            total = summed(first, xs[k], xr[k])
            ys[k][...] = total.astype(BF).reshape(second[0], j, WIDTHS[k])
            spread("y", k, second, ys[k], yr[k], y_ssem.at[k], y_rsem.at[k])
        if k >= 1:
            second = along_y if PATHS[k - 1] == "x" else along_x
            settle("y", "in", k - 1)
            total = summed(second, ys[k - 1], yr[k - 1])
            zr[k - 1][z] = total.astype(BF)
            for i in steps(nz):
                pltpu.make_async_remote_copy(
                    src_ref=zr[k - 1].at[z],
                    dst_ref=zr[k - 1].at[z],
                    send_sem=z_ssem.at[k - 1],
                    recv_sem=z_rsem.at[k - 1],
                    device_id={"grp": (z + i) % nz},
                    device_id_type=MESH,
                ).start()
            owed["z", "in", k - 1] = functools.partial(arrive, zr[k - 1], nz - 1, z_rsem.at[k - 1])
            owed["z", "out", k - 1] = functools.partial(arrive, zr[k - 1], nz - 1, z_ssem.at[k - 1])

    eye_r = lax.broadcasted_iota(I32, (nr, nr), 0) == lax.broadcasted_iota(I32, (nr, nr), 1)
    placed = jnp.concatenate([hot(2, 0, ns), hot(3, 0, ns)], axis=0)
    kept = jnp.where(eye_r, 1.0 - jnp.sum(placed, axis=0, keepdims=True), 0.0)
    place = jnp.concatenate([placed, kept], axis=0).astype(BF)

    def write_layer(layer, buffer, stage, rows):
        stage[...] = buffer[...].reshape(nr * cb, 128).astype(F32)
        for c in range(2):
            for b in range(cb):
                rows[c * ns : (c + 1) * ns, b * 128 : (b + 1) * 128] = stage[
                    pl.ds(c * cb + b, ns, stride=2 * cb), :
                ].astype(BF)
        rows[nr : 2 * nr, :] = hist_v[layer]
        hist_o[layer] = lax.dot_general(
            place, rows[...], (((0,), (0,)), ((), ())), preferred_element_type=F32
        ).astype(BF)
        store = pltpu.make_async_copy(hist_o.at[layer], newhist.at[layer, 0], osem.at[layer])
        store.start()
        owed["store", layer] = store.wait

    settle("push0", "in")
    write_layer(0, push_r0, stage_b, rows1)
    settle("push1", "in")
    write_layer(1, push_r1, stage_c, rows2)

    for k in range(nch):
        settle("z", "in", k)
        total = zr[k][0].astype(F32)
        for i in range(1, nz):
            total += zr[k][i].astype(F32)
        grad[:, starts[k] : starts[k] + WIDTHS[k]] = total
    finish()


def copy_kernel(a, b, a_out, b_out):
    a_out[...] = a[...]
    b_out[...] = b[...]


def per_device(*args):
    x, init, hist, bid, bcnt, hid, hcnt, cols, vals, w1, w2, cot = args
    ns, nz = lax.axis_size("store"), lax.axis_size("grp")
    h = x.shape[-1]
    nx = NX
    ny = ns // (2 * nx)
    j = h // ns
    nr = 2 * ns
    blk = nr // 2
    cb = h // 128
    nch = len(WIDTHS)
    vm = pltpu.VMEM
    dma = pltpu.SemaphoreType.DMA
    slots = vm((ns, 2 * cb, 128), BF)
    stage = vm((nr * cb, 128), F32)
    scratch = [
        vm((nr, h), BF),
        vm((nr, h), BF),
        vm((2, nr, h), BF),
        vm((2, ns), I32),
        vm((1, ns), I32),
        vm((2, ns), I32),
        vm((1, ns), I32),
        vm((2, 4), I32),
        vm((2, 4, blk, blk), BF),
        vm((h, h), BF),
        vm((h, h), BF),
        vm((nr, h), BF),
        vm((ns, 1, 128), I32),
        vm((ns, 1, 128), I32),
        stage,
        stage,
        stage,
        slots,
        slots,
        slots,
        slots,
        slots,
        slots,
        slots,
        slots,
        vm((nr, 2 * nr), BF),
        vm((2 * nr, h), BF),
        vm((2 * nr, h), BF),
        vm((nr, h), BF),
        vm((2, h // 2, nr), BF),
        vm((2, h // 2, nr), BF),
        vm((2, nr, h), BF),
        dma((12,)),
        dma((2, 2)),
        dma((2, 3)),
        dma((2, 2)),
        dma((nch + 1, 2)),
        dma((nch,)),
        dma((nch,)),
        dma((nch,)),
        dma((nch,)),
        dma((nch,)),
        dma((nch,)),
        dma((2,)),
    ]
    scratch += [vm((2, nr, c), BF) for c in WIDTHS]
    sizes = [(nx, ny, c) if p == "x" else (ny, nx, c) for p, c in zip(PATHS, WIDTHS)]
    scratch += [vm((a, b * j, c), BF) for a, b, c in sizes]
    scratch += [vm((a - 1, b * j, c), BF) for a, b, c in sizes]
    scratch += [vm((b, j, c), BF) for a, b, c in sizes]
    scratch += [vm((b - 1, j, c), BF) for a, b, c in sizes]
    scratch += [vm((nz, j, c), BF) for c in WIDTHS]
    results = pl.pallas_call(
        functools.partial(kernel, (ns, nz, ny, nx, h, j)),
        out_shape=(
            jax.ShapeDtypeStruct((2, 1, nr, h), BF),
            jax.ShapeDtypeStruct((j, h), F32),
        ),
        in_specs=[pl.BlockSpec(memory_space=pl.ANY)] * 12,
        out_specs=(
            pl.BlockSpec(memory_space=pl.ANY),
            pl.BlockSpec(memory_space=pltpu.VMEM),
        ),
        scratch_shapes=scratch,
        compiler_params=pltpu.CompilerParams(
            collective_id=0, has_side_effects=True, vmem_limit_bytes=VMEM_BYTES
        ),
        name="gcnii",
    )(
        x,
        init,
        hist,
        jnp.swapaxes(bid, 2, 3),
        bcnt,
        jnp.swapaxes(hid, 2, 3),
        hcnt,
        cols,
        vals,
        w1,
        w2,
        cot,
    )
    specs = (
        pl.BlockSpec((2, 1, nr // 2, h), lambda i: (0, 0, i, 0)),
        pl.BlockSpec((j, h // 2), lambda i: (0, i)),
    )
    return pl.pallas_call(
        copy_kernel,
        grid=(2,),
        out_shape=(
            jax.ShapeDtypeStruct((2, 1, nr, h), BF),
            jax.ShapeDtypeStruct((j, h), F32),
        ),
        in_specs=specs,
        out_specs=specs,
        compiler_params=pltpu.CompilerParams(vmem_limit_bytes=VMEM_BYTES),
        name="write_out",
    )(*results)


def solution(mesh):
    in_specs = (
        P("grp", "store", None, None),
        P("grp", "store", None, None),
        P(None, "grp", "store", None),
        P("grp", "store", None, None),
        P("grp", "store", None),
        P("grp", "store", None, None),
        P("grp", "store", None),
        P("grp", "store", None, None),
        P("grp", "store", None, None, None, None),
        P(),
        P(),
        P("grp", "store", None, None),
    )
    out_specs = (P(None, "grp", "store", None), P("store", None))
    return jax.shard_map(
        per_device, mesh=mesh, in_specs=in_specs, out_specs=out_specs, check_vma=False
    )
```

time: 81.5 us -> 75.5 us (0.926)
  Pallas kernels: 76.8 us -> 73.3 us
  local copies, waits for them, and re-layouts: 3.34 us -> 0 us
    pallas_call x1, Pallas kernels: 76.8 us -> 71.5 us  [per_device(): pl.pallas_call(functools.partial(kernel, (ns, nz, ny, nx, h, j)), out_sha...]
    unnamed x2 -> x0, local copies, waits for them, and re-layouts: 3.34 us -> none
    pallas_call x0 -> x1, Pallas kernels: none -> 1.8 us  [per_device(): pl.pallas_call(copy_kernel, grid=(2,), out_shape=(jax.ShapeDtypeStruct((2...]
where the time goes in v2:
time: 75.5 us; the launch traced here: 74 us
  Pallas kernels  73.3 us (97%)
    pallas_call x1, Pallas kernels, per_device(): pl.pallas_call(functools.partial(kernel, (ns, nz, ny, nx, h, j)), out_sha...  71.5 us
    pallas_call x1, Pallas kernels, per_device(): pl.pallas_call(copy_kernel, grid=(2,), out_shape=(jax.ShapeDtypeStruct((2...  1.8 us

profile of v2, /device:TPU:6, one launch (start us, length us, event | category | flops | bytes accessed | tf_op | source)
XLA Modules:
  0.0 74.0 jit_solution(18403786341711725581)
XLA Ops:
  0.6 71.5 %gcnii.1 = (bf16[2,1,128,1024]{3,2,1,0:T(8,128)(2,1)}, f32[16,1024]{1,0:T(8,128)}) custom-call(bf16[1,1,128,1024]{3,2,1,0:T(8,128)(2,1)} %x_hbm.1, bf16[1,1,128,1024]{3,2,1,0:T(8,128)(2,1)} %init_hbm.1, bf16[2,1,128,1024]{3,2,1,0:T(8,128)(2,1)} %hist_hbm.1, s32[1,1,2,64]{3,2,1,0:T(2,128)} %bitcast.2, s32[1,1,64]{2,1,0:T(1,128)} %bcnt_hbm.1, ...), custom_call_target="tpu_custom_call" | custom-call | tf_op jit(solution)/shard_map/gcnii/pallas_call | solution.py:567
  72.2 1.8 %write_out.1 = (bf16[2,1,128,1024]{3,2,1,0:T(8,128)(2,1)}, f32[16,1024]{1,0:T(8,128)}) custom-call(bf16[2,1,128,1024]{3,2,1,0:T(8,128)(2,1)} %get-tuple-element.4.a, f32[16,1024]{1,0:T(8,128)} %get-tuple-element.5.b), custom_call_target="tpu_custom_call" | custom-call | tf_op jit(solution)/shard_map/write_out/pallas_call | solution.py:601

commit v3 on v2

--- a/solution.py
+++ b/solution.py
@@ -76,6 +76,7 @@
     sup_c,
     s_pair,
     hist_o,
+    grad_v,
     lsem,
     id_sem,
     halo_sem,
@@ -126,9 +127,13 @@
     ]
     loads = [pltpu.make_async_copy(a, b, lsem.at[i]) for i, (a, b) in enumerate(locals_)]
     owed = {}
-    for i, load in enumerate(loads):
-        load.start()
-        owed["load", i] = load.wait
+
+    def begin(first, last):
+        for i in range(first, last):
+            loads[i].start()
+            owed["load", i] = loads[i].wait
+
+    begin(0, 3)
 
     def settle(*name):
         owed.pop(name)()
@@ -147,8 +152,13 @@
         pl.semaphore_signal(barrier, inc=1, device_id={"grp": (z + i) % nz}, device_id_type=MESH)
         return carry
 
-    lax.fori_loop(1, ns, greet_store, 0)
-    lax.fori_loop(1, nz, greet_grp, 0)
+    lax.fori_loop(far_lo, far_hi, greet_store, 0)
+    lax.fori_loop(nz // 4, nz - nz // 4, greet_grp, 0)
+    for low, high in near:
+        lax.fori_loop(low, high, greet_store, 0)
+    lax.fori_loop(1, nz // 4, greet_grp, 0)
+    lax.fori_loop(nz - nz // 4, nz, greet_grp, 0)
+    begin(3, 12)
 
     for i in range(3):
         settle("load", i)
@@ -199,7 +209,7 @@
         owed[name] = functools.partial(arrive, buffer, count, sem)
 
     def push(name, source, target, sems):
-        count = send_all(near + far, source, target, sems.at[0], sems.at[1], False)
+        count = send_all(far + near, source, target, sems.at[0], sems.at[1], False)
         owe((name, "out"), source, count, sems.at[0])
         owe((name, "in"), target, count, sems.at[1])
 
@@ -487,7 +497,11 @@
         total = zr[k][0].astype(F32)
         for i in range(1, nz):
             total += zr[k][i].astype(F32)
-        grad[:, starts[k] : starts[k] + WIDTHS[k]] = total
+        part = pl.ds(starts[k], WIDTHS[k])
+        grad_v[:, part] = total
+        store = pltpu.make_async_copy(grad_v.at[:, part], grad.at[:, part], osem.at[2 + k])
+        store.start()
+        owed["store", 2 + k] = store.wait
     finish()
 
 
@@ -544,6 +558,7 @@
         vm((2, h // 2, nr), BF),
         vm((2, h // 2, nr), BF),
         vm((2, nr, h), BF),
+        vm((j, h), F32),
         dma((12,)),
         dma((2, 2)),
         dma((2, 3)),
@@ -555,7 +570,7 @@
         dma((nch,)),
         dma((nch,)),
         dma((nch,)),
-        dma((2,)),
+        dma((2 + nch,)),
     ]
     scratch += [vm((2, nr, c), BF) for c in WIDTHS]
     sizes = [(nx, ny, c) if p == "x" else (ny, nx, c) for p, c in zip(PATHS, WIDTHS)]
@@ -573,7 +588,7 @@
         in_specs=[pl.BlockSpec(memory_space=pl.ANY)] * 12,
         out_specs=(
             pl.BlockSpec(memory_space=pl.ANY),
-            pl.BlockSpec(memory_space=pltpu.VMEM),
+            pl.BlockSpec(memory_space=pl.ANY),
         ),
         scratch_shapes=scratch,
         compiler_params=pltpu.CompilerParams(

time: 75.5 us -> 74.1 us (0.981)
  Pallas kernels: 73.3 us -> 72.2 us
    pallas_call x1, Pallas kernels: 71.5 us -> 70.4 us  [per_device(): pl.pallas_call(functools.partial(kernel, (ns, nz, ny, nx, h, j)), out_sha...]
where the time goes in v3:
time: 74.1 us; the launch traced here: 72.8 us
  Pallas kernels  72.2 us (97%)
    pallas_call x1, Pallas kernels, per_device(): pl.pallas_call(functools.partial(kernel, (ns, nz, ny, nx, h, j)), out_sha...  70.4 us
    pallas_call x1, Pallas kernels, per_device(): pl.pallas_call(copy_kernel, grid=(2,), out_shape=(jax.ShapeDtypeStruct((2...  1.8 us

profile of v3, /device:TPU:6, one launch (start us, length us, event | category | flops | bytes accessed | tf_op | source)
XLA Modules:
  0.0 72.8 jit_solution(7609147938235226652)
XLA Ops:
  0.6 70.4 %gcnii.1 = (bf16[2,1,128,1024]{3,2,1,0:T(8,128)(2,1)}, f32[16,1024]{1,0:T(8,128)}) custom-call(bf16[1,1,128,1024]{3,2,1,0:T(8,128)(2,1)} %x_hbm.1, bf16[1,1,128,1024]{3,2,1,0:T(8,128)(2,1)} %init_hbm.1, bf16[2,1,128,1024]{3,2,1,0:T(8,128)(2,1)} %hist_hbm.1, s32[1,1,2,64]{3,2,1,0:T(2,128)} %bitcast.2, s32[1,1,64]{2,1,0:T(1,128)} %bcnt_hbm.1, ...), custom_call_target="tpu_custom_call" | custom-call | tf_op jit(solution)/shard_map/gcnii/pallas_call | solution.py:582
  71.0 1.8 %write_out.1 = (bf16[2,1,128,1024]{3,2,1,0:T(8,128)(2,1)}, f32[16,1024]{1,0:T(8,128)}) custom-call(bf16[2,1,128,1024]{3,2,1,0:T(8,128)(2,1)} %get-tuple-element.4.a, f32[16,1024]{1,0:T(8,128)} %get-tuple-element.5.b), custom_call_target="tpu_custom_call" | custom-call | tf_op jit(solution)/shard_map/write_out/pallas_call | solution.py:616

commit v4 on v3

--- a/solution.py
+++ b/solution.py
@@ -15,7 +15,7 @@
 GELU_C = 0.044715
 MESH = pl.DeviceIdType.MESH
 NX = 4
-WIDTHS = (256, 256, 256, 256)
+WIDTHS = (256, 384, 256, 128)
 PATHS = "xxxx"
 FAR_FIRST = 1
 CW = 256

time: 74.1 us -> 75.6 us (1.020)
  Pallas kernels: 72.2 us -> 73.8 us
    pallas_call x1, Pallas kernels: 70.4 us -> 72 us  [per_device(): pl.pallas_call(functools.partial(kernel, (ns, nz, ny, nx, h, j)), out_sha...]
where the time goes in v4:
time: 75.6 us; the launch traced here: 74.5 us
  Pallas kernels  73.8 us (98%)
    pallas_call x1, Pallas kernels, per_device(): pl.pallas_call(functools.partial(kernel, (ns, nz, ny, nx, h, j)), out_sha...  72 us
    pallas_call x1, Pallas kernels, per_device(): pl.pallas_call(copy_kernel, grid=(2,), out_shape=(jax.ShapeDtypeStruct((2...  1.8 us

profile of v4, /device:TPU:6, one launch (start us, length us, event | category | flops | bytes accessed | tf_op | source)
XLA Modules:
  0.0 74.5 jit_solution(5470889482256893276)
XLA Ops:
  0.6 72.0 %gcnii.1 = (bf16[2,1,128,1024]{3,2,1,0:T(8,128)(2,1)}, f32[16,1024]{1,0:T(8,128)}) custom-call(bf16[1,1,128,1024]{3,2,1,0:T(8,128)(2,1)} %x_hbm.1, bf16[1,1,128,1024]{3,2,1,0:T(8,128)(2,1)} %init_hbm.1, bf16[2,1,128,1024]{3,2,1,0:T(8,128)(2,1)} %hist_hbm.1, s32[1,1,2,64]{3,2,1,0:T(2,128)} %bitcast.2, s32[1,1,64]{2,1,0:T(1,128)} %bcnt_hbm.1, ...), custom_call_target="tpu_custom_call" | custom-call | tf_op jit(solution)/shard_map/gcnii/pallas_call | solution.py:582
  72.7 1.8 %write_out.1 = (bf16[2,1,128,1024]{3,2,1,0:T(8,128)(2,1)}, f32[16,1024]{1,0:T(8,128)}) custom-call(bf16[2,1,128,1024]{3,2,1,0:T(8,128)(2,1)} %get-tuple-element.4.a, f32[16,1024]{1,0:T(8,128)} %get-tuple-element.5.b), custom_call_target="tpu_custom_call" | custom-call | tf_op jit(solution)/shard_map/write_out/pallas_call | solution.py:616
